TPU v7x, 32 devices: a whole 2x2x4 slice. The times are simulated.
32 devices in a mesh: wave: 8 (over z, x), band: 4 (over y, core).
Axes of the slice: x: 2, y: 2, z: 4, core: 2. Of those that a mesh axis runs over, the one named last changes fastest.
Arguments:
- spectral: bfloat16 [1920, 2, 128, 1280], P('wave', None, 'band'), may hold values from -0.0059814453 to 0.0059814453
- legendre: bfloat16 [1920, 8, 1280], P('wave'), may hold values from -4 to 4
- slot_wave: int32 [1920], replicated, may hold values from 0 to 1280, as said below
- lat_points: int32 [8], P('wave'), may hold values from 20 to 5136, as said below
- level_mix: float32 [32, 32], replicated, may hold values from -1 to 1
- grid_scale: float32 [8, 5632], P('wave', 'band'), may hold values from 0.5 to 2
- gauss_w: float32 [8], replicated, may hold values from 2 to 8
Outputs:
- grid_out: float32 [128, 8, 5632], P(None, 'wave', 'band')
- spec_out: bfloat16 [1920, 2, 128, 1280], P('wave', None, 'band')
Inputs may be any that keep to these rules, and one draw needn't show every extreme that they name: `slot_wave`: every wavenumber 0 to 1279 is held by exactly one slot; all other slots hold 1280; some index of wave has all 240 of its slots holding wavenumbers. `lat_points`: each value is 20 + 4 i for a latitude row i from 0 to 1279; some latitude has 5136 points.
All inputs are finite; a program needn't handle non-finite values.
Results may differ from a plain program's by a relative error of at most 0.0062.
Values may be sent and summed in bfloat16 or wider, within the bound.
A program may use at most 192 MiB of HBM per device.

v0:
```python
import math

import jax
import jax.numpy as jnp
from jax import lax
from jax.sharding import PartitionSpec as P

M = 1280
NLEV = 32


TWO_PI = 2.0 * math.pi


def trig_table(wave_ids, points, lon_first, lon_width):
    lon_index = lon_first + jnp.arange(lon_width, dtype=jnp.int32)
    turn_index = wave_ids[None, :, None] * lon_index[None, None, :] % points[:, None, None]
    angle_rad = (
        turn_index.astype(jnp.float32) * (TWO_PI / points.astype(jnp.float32))[:, None, None]
    )
    return jnp.stack([jnp.cos(angle_rad), jnp.sin(angle_rad)], axis=2)


def valid_waves(wave_ids, points):
    return ((wave_ids[None, :] < M) & (2 * wave_ids[None, :] < points[:, None])).astype(jnp.float32)


def lon_mask(points, lon_first, lon_width):
    lon_index = lon_first + jnp.arange(lon_width, dtype=jnp.int32)
    return (lon_index[None, :] < points[:, None]).astype(jnp.float32)


def inverse_terms(four_coef, wave_ids, points, lon_first, lon_width):
    valid_wave = valid_waves(wave_ids, points)
    doubled = jnp.where(wave_ids == 0, 1.0, 2.0).astype(jnp.float32)
    sign_pair = jnp.array([1.0, -1.0], jnp.float32)
    factor = (valid_wave * doubled[None, :])[:, :, None] * sign_pair
    weighted = four_coef.astype(jnp.float32) * jnp.transpose(factor, (1, 2, 0))[:, :, None, :]
    trig_tab = trig_table(wave_ids, points, lon_first, lon_width)
    grid_rows = jnp.einsum("scfa,ascj->faj", weighted, trig_tab, precision=lax.Precision.HIGHEST)
    return grid_rows * lon_mask(points, lon_first, lon_width)[None]


def direct_terms(grid_rows, wave_ids, points, lon_first, lon_width):
    valid_wave = valid_waves(wave_ids, points)
    sign_pair = jnp.array([1.0, -1.0], jnp.float32)
    trig_tab = trig_table(wave_ids, points, lon_first, lon_width)
    masked_rows = grid_rows * lon_mask(points, lon_first, lon_width)[None]
    summed = jnp.einsum("faj,ascj->fsca", masked_rows, trig_tab, precision=lax.Precision.HIGHEST)
    factor = valid_wave[:, :, None] * sign_pair / points.astype(jnp.float32)[:, None, None]
    return summed * jnp.transpose(factor, (1, 2, 0))[None]


def mix_levels(grid_rows, level_mix, grid_scale):
    fields, lats, lons = grid_rows.shape
    stacked = grid_rows.reshape(fields // NLEV, NLEV, lats, lons)
    mixed_grid = jnp.einsum("ik,bkaj->biaj", level_mix, stacked, precision=lax.Precision.HIGHEST)
    return mixed_grid.reshape(fields, lats, lons) * grid_scale[None]


def body(spectral, legendre, slot_wave, lat_points, level_mix, grid_scale, gauss_w):
    slot_count = spectral.shape[0]
    wave_here = lax.dynamic_slice_in_dim(slot_wave, lax.axis_index("wave") * slot_count, slot_count)
    degree = jnp.arange(spectral.shape[3], dtype=jnp.int32)
    keep_mask = degree[None, :] >= wave_here[:, None]
    masked = jnp.where(keep_mask[:, None, None, :], spectral, jnp.zeros((), jnp.bfloat16))
    four_coef = jnp.einsum(
        "scfn,sln->scfl", masked, legendre, preferred_element_type=jnp.float32
    ).astype(jnp.bfloat16)
    fourier = lax.all_to_all(four_coef, "wave", split_axis=3, concat_axis=0, tiled=True)
    lon_width = grid_scale.shape[1]
    lon_first = lax.axis_index("band") * lon_width
    grid_rows = inverse_terms(
        lax.all_gather(fourier, "band", axis=2, tiled=True),
        slot_wave,
        lat_points,
        lon_first,
        lon_width,
    )
    mixed_grid = mix_levels(grid_rows, level_mix, grid_scale)
    back_coef = lax.psum_scatter(
        direct_terms(mixed_grid, slot_wave, lat_points, lon_first, lon_width),
        "band",
        scatter_dimension=0,
        tiled=True,
    )
    fourier_back = lax.all_to_all(
        back_coef.astype(jnp.bfloat16), "wave", split_axis=1, concat_axis=3, tiled=True
    )
    fourier_back = lax.optimization_barrier(fourier_back)
    weighted = (fourier_back.astype(jnp.float32) * gauss_w[None, None, None, :]).astype(
        jnp.bfloat16
    )
    summed = jnp.einsum("fscl,sln->scfn", weighted, legendre, preferred_element_type=jnp.float32)
    spec_out = jnp.where(keep_mask[:, None, None, :], summed, 0.0).astype(jnp.bfloat16)
    return (grid_rows, spec_out)


def solution(mesh):
    placed = (
        P("wave", None, "band", None),
        P("wave", None, None),
        P(),
        P("wave"),
        P(),
        P("wave", "band"),
        P(),
    )
    return jax.shard_map(
        body,
        mesh=mesh,
        in_specs=placed,
        out_specs=(P(None, "wave", "band"), P("wave", None, "band", None)),
        check_vma=False,
    )
```

profile of v0, /device:TPU:0, one launch (start us, length us, event | category | flops | bytes accessed | tf_op | source)
XLA Modules:
  0.0 319.5 jit_solution(7774434579813613560)
XLA Ops:
  0.6 0.0 copy-start
  0.7 0.8 dynamic_slice.3
  1.4 0.2 iota_compare_fusion
  1.7 0.0 copy-start.5
  1.7 0.0 copy-start.1
  1.7 0.0 copy-start.2
  1.7 30.9 %fusion.23 = bf16[240,2,32,8]{2,3,1,0:T(8,128)(2,1)S(1)} fusion(bf16[240,8,1280]{2,1,0:T(8,128)(2,1)} %param.12, bf16[240,2,32,1280]{3,2,1,0:T(8,128)(2,1)} %param.11, pred[240,1280]{1,0:T(8,128)(4,1)S(1)} %iota_compare_fusion), kind=kOutput, calls=%fused_computation.30 | convolution fusion | flops 334356480 | bytes 44789760 | tf_op jit(solution)/shard_map/scfn,sln->scfl/dot_general | solution.py:67
  32.6 1.5 copy.16
  34.1 7.8 %all-to-all-start = ((bf16[240,2,32,8]{0,2,1,3:T(8,128)(2,1)}), bf16[240,2,32,8]{0,2,1,3:T(8,128)(2,1)S(1)}, u32[]{:S(2)}, u32[]{:S(2)}) async-start(bf16[240,2,32,8]{0,2,1,3:T(8,128)(2,1)} %copy.16), calls=%async_computation | async-start | bytes 524288 | tf_op jit(solution)/shard_map/all_to_all | solution.py:70
  42.6 0.6 dynamic-slice
  44.0 0.0 copy-start.4
  44.0 145.3 %cosine_bitcast_fusion = (f32[1,1920,1,1408]{3,1,2,0:T(8,128)}, f32[1,1920,1,1408]{3,1,2,0:T(8,128)}) fusion(s32[]{:T(128)} %bitcast.1, f32[]{:T(128)} %bitcast.3, s32[1408]{0:T(1024)S(1)} %iota_add_fusion, s32[1920]{0:T(1024)S(1)} %copy-done.1, pred[]{:T(512)} %bitcast.2), kind=kLoop, calls=%fused_computation.13 | loop fusion | flops 27033600 | bytes 21640200 | tf_op jit(solution)/shard_map/stack | solution.py:21
  189.3 0.1 multiply_divide_fusion
  189.4 0.2 copy.17
  189.5 0.3 all_to_all.29
  189.8 0.0 slice-start
  189.8 10.0 %all_gather.3 = bf16[1920,2,128,1]{0,2,1,3:T(8,128)(2,1)S(1)} all-gather(bf16[1920,2,32,1]{0,2,1,3:T(8,128)(2,1)S(1)} %all_to_all.29), channel_id=1, replica_groups=mesh['wave'=8,'band'=4] {'band'}, dimensions={2}, use_global_device_ids=true | all-gather | bytes 1228800 | tf_op jit(solution)/shard_map/all_gather | solution.py:74
  199.8 18.1 %fusion.19 = f32[1,1408,128]{1,2,0:T(8,128)S(1)} fusion(f32[1,1920,1,1408]{3,1,2,0:T(8,128)} %get-tuple-element.10, f32[1,1920,1,1408]{3,1,2,0:T(8,128)} %get-tuple-element.9, bf16[1920,2,128,1]{0,2,1,3:T(8,128)(2,1)S(1)} %all_gather.3, f32[1920,2]{0,1:T(2,128)S(1)} %get-tuple-element.12, f32[1408]{0:T(1024)S(1)} %compare_convert_fusion), kind=kOutput, calls=%fused_computation.25 | convolution fusion | flops 8311291904 | bytes 23351808 | tf_op jit(solution)/shard_map/scfa,ascj->faj/dot_general | solution.py:40
  218.0 0.7 fusion.35
  218.8 21.4 %fusion.17 = f32[128,1920,2,1]{0,1,2,3:T(8,128)S(1)} fusion(f32[1,1920,1,1408]{3,1,2,0:T(8,128)} %get-tuple-element.10, f32[1,1920,1,1408]{3,1,2,0:T(8,128)S(1)} %bitcast.90, f32[1920,2]{0,1:T(2,128)S(1)} %get-tuple-element.11, f32[128,1,1,1,1,1,1408]{6,0,5,4,3,2,1:T(8,128)S(1)} %bitcast.94, f32[1408]{0:T(1024)S(1)} %compare_convert_fusion, f32[1408]{0:T(1024)S(1)} %reduce), kind=kOutput, calls=%fused_computation.23 | convolution fusion | flops 8310980608 | bytes 24340480 | tf_op jit(solution)/shard_map/faj,ascj->fsca/dot_general | solution.py:49
  240.2 0.0 copy-start.3
  240.2 2.4 copy.18
  242.6 39.3 %all-reduce.2 = bf16[128,1920,2,1]{1,2,3,0:T(2,128)(2,1)S(1)} all-reduce(f32[128,1920,2,1]{1,2,3,0:T(2,128)} %copy.18), channel_id=2, replica_groups=mesh['wave'=8,'band'=4] {'band'}, use_global_device_ids=true, to_apply=%region_0.2.clone | all-reduce | flops 491520 | bytes 2949120
  281.9 0.2 dynamic-slice_convert_fusion
  282.1 1.3 copy.19
  283.4 1.4 reshape.286
  284.7 6.0 %all-to-all-start.1 = ((bf16[8,2,7680]{2,1,0:T(2,128)(2,1)}), bf16[8,2,7680]{2,1,0:T(2,128)(2,1)S(1)}, u32[]{:S(2)}, u32[]{:S(2)}) async-start(bf16[8,2,7680]{2,1,0:T(2,128)(2,1)} %reshape.286), calls=%async_computation.1 | async-start | bytes 491520 | tf_op jit(solution)/shard_map/all_to_all | solution.py:87
  290.7 1.6 copy.21
  292.3 7.4 %all-to-all-done.1 = bf16[8,2,7680]{2,1,0:T(2,128)(2,1)S(1)} async-done(((bf16[8,2,7680]{2,1,0:T(2,128)(2,1)}), bf16[8,2,7680]{2,1,0:T(2,128)(2,1)S(1)}, u32[]{:S(2)}, u32[]{:S(2)}) %all-to-all-start.1) | async-done | bytes 245792 | tf_op jit(solution)/shard_map/all_to_all | solution.py:87
  299.7 0.5 reshape.287
  300.2 0.6 copy.24
  300.9 18.3 %fusion.3 = bf16[240,2,32,1280]{3,2,1,0:T(8,128)(2,1)} fusion(pred[240,1280]{1,0:T(8,128)(4,1)S(1)} %iota_compare_fusion, bf16[240,8,1280]{2,1,0:T(8,128)(2,1)} %param.12, bf16[32,240,2,8]{0,3,2,1:T(8,128)(2,1)S(1)} %bitcast.91, f32[8]{0:T(128)S(1)} %copy-done.3), kind=kOutput, calls=%fused_computation.4 | convolution fusion | flops 354263040 | bytes 44789792 | tf_op jit(solution)/shard_map/fscl,sln->scfn/dot_general | solution.py:94
  (18 shorter events, 0.1 us)
Async XLA Ops:
  0.6 217.3 %copy-start = (f32[32,32]{1,0:T(8,128)S(1)}, f32[32,32]{1,0:T(8,128)}, u32[]{:S(2)}) copy-start(f32[32,32]{1,0:T(8,128)} %param.15) | copy-start | bytes 12292
  1.7 40.9 %copy-start.5 = (u32[32]{0:T(128)S(1)}, u32[32]{0:T(128)}, u32[]{:S(2)}) copy-start(u32[32]{0:T(128)} %constant.46) | copy-start | bytes 388
  1.7 42.2 %copy-start.1 = (s32[1920]{0:T(1024)S(1)}, s32[1920]{0:T(1024)}, u32[]{:S(2)}) copy-start(s32[1920]{0:T(1024)} %param.13) | copy-start | bytes 23044
  1.7 42.2 %copy-start.2 = (f32[1,1408]{1,0:T(1,128)S(1)}, f32[1,1408]{1,0:T(1,128)}, u32[]{:S(2)}) copy-start(f32[1,1408]{1,0:T(1,128)} %param.16) | copy-start | bytes 16900
  34.1 155.3 %all-to-all-start = ((bf16[240,2,32,8]{0,2,1,3:T(8,128)(2,1)}), bf16[240,2,32,8]{0,2,1,3:T(8,128)(2,1)S(1)}, u32[]{:S(2)}, u32[]{:S(2)}) async-start(bf16[240,2,32,8]{0,2,1,3:T(8,128)(2,1)} %copy.16), calls=%async_computation | async-start | bytes 524288 | tf_op jit(solution)/shard_map/all_to_all | solution.py:70
  44.0 145.3 %copy-start.4 = (f32[2]{0:T(128)S(1)}, f32[2]{0:T(128)}, u32[]{:S(2)}) copy-start(f32[2]{0:T(128)} %constant.41.clone) | copy-start | bytes 28
  189.8 28.9 %slice-start = ((s8[10813440]{0:T(1024)(128)(4,1)}), s8[4194304]{0:T(1024)(128)(4,1)S(1)}, s32[]{:S(2)}) async-start(s8[10813440]{0:T(1024)(128)(4,1)} %bitcast.89), calls=%async_computation.2 | async-start | bytes 8388608
  199.8 18.9 %slice-start.1 = ((s8[10813440]{0:T(1024)(128)(4,1)}), s8[4194304]{0:T(1024)(128)(4,1)S(1)}, s32[]{:S(2)}) async-start(s8[10813440]{0:T(1024)(128)(4,1)} %bitcast.89), calls=%async_computation.3 | async-start | bytes 8388608
  199.8 18.9 %slice-start.2 = ((s8[10813440]{0:T(1024)(128)(4,1)}), s8[2424832]{0:T(1024)(128)(4,1)S(1)}, s32[]{:S(2)}) async-start(s8[10813440]{0:T(1024)(128)(4,1)} %bitcast.89), calls=%async_computation.4 | async-start | bytes 4849664
  240.2 60.7 %copy-start.3 = (f32[8]{0:T(128)S(1)}, f32[8]{0:T(128)}, u32[]{:S(2)}) copy-start(f32[8]{0:T(128)} %param.17) | copy-start | bytes 100
  284.7 15.0 %all-to-all-start.1 = ((bf16[8,2,7680]{2,1,0:T(2,128)(2,1)}), bf16[8,2,7680]{2,1,0:T(2,128)(2,1)S(1)}, u32[]{:S(2)}, u32[]{:S(2)}) async-start(bf16[8,2,7680]{2,1,0:T(2,128)(2,1)} %reshape.286), calls=%async_computation.1 | async-start | bytes 491520 | tf_op jit(solution)/shard_map/all_to_all | solution.py:87
where the time goes:
time: 325 us; the launch traced here: 319 us
  other arithmetic  146 us (45%)
  matrix products  89.5 us (28%)
  blocking collectives  49.3 us (15%)
  starting transfers between devices  13.8 us (4%)
  local copies, waits for them, and re-layouts  11.3 us (3%)
  waiting for transfers between devices  7.37 us (2%)
    another operation x1, other arithmetic, trig_table(): return jnp.stack([jnp.cos(angle_rad), jnp.sin(angle_rad)], axis=2)  145 us
    unnamed x1, blocking collectives  39.3 us
    dot_general x1, matrix products, body(): jnp.einsum('scfn,sln->scfl', masked, legendre, preferred_element_type=jnp...  30.9 us
    dot_general x1, matrix products, direct_terms(): jnp.einsum('faj,ascj->fsca', masked_rows, trig_tab, precision=lax.Precisi...  21.4 us
    dot_general x1, matrix products, body(): jnp.einsum('fscl,sln->scfn', weighted, legendre, preferred_element_type=j...  18.3 us
    dot_general x1, matrix products, inverse_terms(): jnp.einsum('scfa,ascj->faj', weighted, trig_tab, precision=lax.Precision....  18.1 us
    all_gather x1, blocking collectives, body(): lax.all_gather(fourier, 'band', axis=2, tiled=True)  10 us
    all_to_all x1, starting transfers between devices, body(): lax.all_to_all(four_coef, 'wave', split_axis=3, concat_axis=0, tiled=True)  7.79 us
  transfers between devices with their start and end apart: 2, of which 1 were waited for; matrix products, arithmetic and copies ran while one was open for 46% of the time, Pallas kernels for 0%

commit v1 on v0

v1 whole, which is shorter than its diff:
```python
import math

import jax
import jax.numpy as jnp
from jax import lax
from jax.experimental import pallas as pl
from jax.experimental.pallas import tpu as pltpu
from jax.sharding import PartitionSpec as P

TWO_PI = 2.0 * math.pi
VMEM_LIMIT = 56 * 1024 * 1024
NT = (((1,), (1,)), ((), ()))
NN = (((1,), (0,)), ((), ()))


def dot(a, b, dims):
    return lax.dot_general(a, b, dims, preferred_element_type=jnp.float32)


def masked_legendre(leg_ref, thr_ref):
    rows, degrees = leg_ref.shape
    degree = lax.broadcasted_iota(jnp.int32, (rows, degrees), 1)
    keep = degree >= thr_ref[...][:, :1]
    return jnp.where(keep, leg_ref[...].astype(jnp.float32), 0.0).astype(jnp.bfloat16)


def forward_kernel(lats, spec_ref, leg_ref, thr_ref, out_ref):
    slots, pairs, degrees = spec_ref.shape
    legm = masked_legendre(leg_ref, thr_ref)
    lane_slot = lax.broadcasted_iota(jnp.int32, (pairs, slots * lats), 1) // lats
    total = jnp.zeros((pairs, slots * lats), jnp.float32)
    step = 4
    for first in range(0, slots, step):
        block = spec_ref[first : first + step].reshape(step * pairs, degrees)
        res = dot(block, legm, NT)
        for k in range(step):
            total = jnp.where(lane_slot == first + k, res[k * pairs : (k + 1) * pairs], total)
    out_ref[...] = total.astype(jnp.bfloat16)


def backward_kernel(lats, coef_ref, leg_ref, thr_ref, out_ref):
    slots, pairs, degrees = out_ref.shape
    legm = masked_legendre(leg_ref, thr_ref)
    lane_slot = lax.broadcasted_iota(jnp.int32, (pairs, slots * lats), 1) // lats
    coef = coef_ref[...].astype(jnp.float32)
    step = 4
    for first in range(0, slots, step):
        lhs = jnp.concatenate(
            [jnp.where(lane_slot == first + k, coef, 0.0) for k in range(step)], axis=0
        ).astype(jnp.bfloat16)
        res = dot(lhs, legm, NN).astype(jnp.bfloat16)
        out_ref[first : first + step] = res.reshape(step, pairs, degrees)


def turn(product, points, inverse):
    whole = jnp.round(product * inverse)
    x = (product - whole * points) * inverse * TWO_PI
    y = x * x
    c = 1.0
    for k in range(9, 0, -1):
        c = 1.0 - c * y * (1.0 / ((2 * k - 1) * (2 * k)))
    s = 1.0
    for k in range(9, 0, -1):
        s = 1.0 - s * y * (1.0 / ((2 * k) * (2 * k + 1)))
    return c, s * x


def table_kernel(lanes, wave_ref, points_ref, out_ref):
    rows = out_ref.shape[0]
    slots = wave_ref.shape[1]
    points = points_ref[0].astype(jnp.float32)
    inverse = 1.0 / jnp.full((1, 1), points, jnp.float32)
    for start in range(0, slots, lanes):
        here = pl.ds(start, lanes)
        there = pl.ds(slots + start, lanes)
        wave = wave_ref[:, here].astype(jnp.float32)
        lon = lax.broadcasted_iota(jnp.int32, (16, lanes), 0).astype(jnp.float32)
        c0, s0 = turn(wave * lon, points, inverse)
        cr, sr = turn(jnp.broadcast_to(wave, (8, lanes)) * 16.0, points, inverse)
        cr = jnp.concatenate([cr, cr], axis=0)
        sr = jnp.concatenate([sr, sr], axis=0)

        def step(i, held):
            c, s = held
            at = pl.ds(pl.multiple_of(i * 16, 16), 16)
            out_ref[at, here] = c.astype(jnp.bfloat16)
            out_ref[at, there] = s.astype(jnp.bfloat16)
            return c * cr - s * sr, s * cr + c * sr

        lax.fori_loop(0, rows // 16, step, (c0, s0), unroll=2)


def grid_kernel(
    levels, coef_ref, table_ref, wave_ref, points_ref, mix_ref, scale_ref,
    grid_ref, back_ref, canvas, groups, sums,
):
    fields = coef_ref.shape[0] // 2
    rows = table_ref.shape[0]
    slots = wave_ref.shape[1]
    lons = grid_ref.shape[1]
    points = points_ref[0]
    quarter = points // 4
    wave = wave_ref[...]
    rest = wave & 3
    valid = jnp.where(2 * wave < points, 1.0, 0.0)
    odd = (rest & 1).astype(jnp.float32)
    even = 1.0 - odd
    sign_even = even * (1.0 - rest.astype(jnp.float32))
    sign_odd = odd * (rest.astype(jnp.float32) - 2.0)
    factor = valid * jnp.where(wave == 0, 1.0, 2.0)
    a = coef_ref[:fields].astype(jnp.float32) * factor
    b = coef_ref[fields:].astype(jnp.float32) * factor
    low, high = pl.ds(0, slots), pl.ds(slots, slots)
    for k, (to_cos, to_sin) in enumerate(
        ((a * even, -b * even), (a * odd, -b * odd), (a * sign_even, -b * sign_even), (b * sign_odd, a * sign_odd))
    ):
        at = pl.ds(k * fields, fields)
        groups[at, low] = to_cos.astype(jnp.bfloat16)
        groups[at, high] = to_sin.astype(jnp.bfloat16)

    part = rows // 4

    @pl.loop(0, 4)
    def _(i):
        at = pl.ds(pl.multiple_of(i * part, 16), part)
        sums[at, :] = dot(table_ref[at, :], groups[...], NT)

    ga = sums[:, 0 * fields : 1 * fields]
    gb = sums[:, 1 * fields : 2 * fields]
    gc = sums[:, 2 * fields : 3 * fields]
    gd = sums[:, 3 * fields : 4 * fields]
    for r, x in enumerate((ga + gb, gc + gd, ga - gb, gc - gd)):
        canvas[pl.ds(r * quarter, rows), :] = x

    tile = 128

    @pl.loop(0, lons // tile)
    def _(i):
        at = pl.ds(pl.multiple_of(i * tile, tile), tile)
        lon = i * tile + lax.broadcasted_iota(jnp.int32, (tile, fields), 0)
        g = jnp.where(lon < points, canvas[at, :], 0.0)
        grid_ref[:, at] = g.T.astype(jnp.bfloat16)
        gl = g.astype(jnp.bfloat16)
        mixed = [
            dot(gl[:, f : f + levels], mix_ref[...], NT) for f in range(0, fields, levels)
        ]
        mixed = mixed[0] if len(mixed) == 1 else jnp.concatenate(mixed, axis=1)
        canvas[at, :] = mixed * scale_ref[at, :]

    inside = lax.broadcasted_iota(jnp.int32, (rows, fields), 0) < quarter
    y = [jnp.where(inside, canvas[pl.ds(r * quarter, rows), :], 0.0) for r in range(4)]
    p, q, v, w = y[0] + y[2], y[1] + y[3], y[0] - y[2], y[1] - y[3]
    sums[:, 0 * fields : 1 * fields] = p + q
    sums[:, 1 * fields : 2 * fields] = p - q
    sums[:, 2 * fields : 3 * fields] = v
    sums[:, 3 * fields : 4 * fields] = w
    u = sums[...].T.astype(jnp.bfloat16)
    over = 1.0 / jnp.full((1, 1), points.astype(jnp.float32), jnp.float32)
    width = 512 if slots % 512 == 0 else 128

    @pl.loop(0, slots // width)
    def _(i):
        at = pl.ds(pl.multiple_of(i * width, width), width)
        to = pl.ds(pl.multiple_of(slots + i * width, width), width)
        zc = dot(u, table_ref[:, at], NN)
        zs = dot(u, table_ref[:, to], NN)
        wv = wave_ref[:, at]
        rs = wv & 3
        gain = jnp.where(2 * wv < points, 1.0, 0.0) * over
        sg = jnp.where(rs == 1, -1.0, 1.0)
        f0, f1, f2, f3 = (slice(k * fields, (k + 1) * fields) for k in range(4))
        is0, is2 = rs == 0, rs == 2
        re = jnp.where(is0, zc[f0], jnp.where(is2, zc[f1], zc[f2] + sg * zs[f3]))
        im = jnp.where(is0, -zs[f0], jnp.where(is2, -zs[f1], sg * zc[f3] - zs[f2]))
        back_ref[0:fields, at] = (re * gain).astype(jnp.bfloat16)
        back_ref[fields : 2 * fields, at] = (im * gain).astype(jnp.bfloat16)


def params():
    return pltpu.CompilerParams(vmem_limit_bytes=VMEM_LIMIT)


def whole():
    return pl.BlockSpec(memory_space=pltpu.VMEM)


def scalar():
    return pl.BlockSpec(memory_space=pltpu.SMEM)


def make_table(wave_row, points, rows):
    slots = wave_row.shape[1]
    return pl.pallas_call(
        lambda *refs: table_kernel(512 if slots % 512 == 0 else 128, *refs),
        out_shape=jax.ShapeDtypeStruct((rows, 2 * slots), jnp.bfloat16),
        in_specs=[whole(), scalar()],
        out_specs=whole(),
        compiler_params=params(),
        cost_estimate=pl.CostEstimate(
            flops=16 * rows * slots, bytes_accessed=4 * rows * slots, transcendentals=0
        ),
        name="trig_table",
    )(wave_row, points)


def on_grid(levels, coef, table, wave_row, points, mix, scale_cols, lons):
    pairs, slots = coef.shape
    fields = pairs // 2
    rows = table.shape[0]
    return pl.pallas_call(
        lambda *refs: grid_kernel(levels, *refs),
        out_shape=(
            jax.ShapeDtypeStruct((fields, lons), jnp.bfloat16),
            jax.ShapeDtypeStruct((pairs, slots), jnp.bfloat16),
        ),
        in_specs=[whole(), whole(), whole(), scalar(), whole(), whole()],
        out_specs=(whole(), whole()),
        scratch_shapes=[
            pltpu.VMEM((lons + rows, fields), jnp.float32),
            pltpu.VMEM((4 * fields, 2 * slots), jnp.bfloat16),
            pltpu.VMEM((rows, 4 * fields), jnp.float32),
        ],
        compiler_params=params(),
        cost_estimate=pl.CostEstimate(
            flops=4 * rows * 2 * slots * 4 * fields,
            bytes_accessed=4 * rows * slots,
            transcendentals=0,
        ),
        name="grid_step",
    )(coef, table, wave_row, points, mix, scale_cols)


def block_slots(slots, lats):
    for count in (16, 8, 4):
        if slots % count == 0 and (count * lats) % 128 == 0:
            return count
    return 0


def body(spectral, legendre, slot_wave, lat_points, level_mix, grid_scale, gauss_w):
    slots, _, fields, degrees = spectral.shape
    lats = legendre.shape[1]
    levels = level_mix.shape[0]
    pairs = 2 * fields
    waves = slot_wave.shape[0] // slots
    bands = lax.axis_size("band")
    lon_width = grid_scale.shape[1]
    lons = lon_width * bands
    rows = -(-lons // 512) * 128
    wave_here = lax.dynamic_slice_in_dim(slot_wave, lax.axis_index("wave") * slots, slots)
    count = block_slots(slots, lats)
    empty = degrees

    padded = -(-slots // 128) * 128 if slots >= 128 else slots
    spread = jnp.pad(
        slot_wave.reshape(waves, slots), ((0, 0), (0, padded - slots)), constant_values=empty
    ).reshape(1, waves * padded)
    total = -(-(waves * padded) // 512) * 512
    wave_row = jnp.pad(spread, ((0, 0), (0, total - waves * padded)), constant_values=empty)
    wave_row = jnp.where(wave_row >= empty, 4 * lons, wave_row)
    table_wave = jnp.where(wave_row >= 4 * lons, 0, wave_row)
    scale_all = lax.all_gather(grid_scale, "band", axis=1, tiled=True)

    if count:
        thr = jnp.broadcast_to(wave_here[:, None, None], (slots, lats, 128)).reshape(-1, 128)
        leg_rows = legendre.reshape(slots * lats, degrees)
        block = count * lats
        legendre_cost = pl.CostEstimate(
            flops=2 * slots * pairs * degrees * block,
            bytes_accessed=2 * slots * (pairs + lats) * degrees,
            transcendentals=0,
        )
        leg_specs = [
            pl.BlockSpec((block, degrees), lambda i: (i, 0)),
            pl.BlockSpec((block, 128), lambda i: (i, 0)),
        ]
        coef = pl.pallas_call(
            lambda *refs: forward_kernel(lats, *refs),
            grid=(slots // count,),
            out_shape=jax.ShapeDtypeStruct((pairs, slots * lats), jnp.bfloat16),
            in_specs=[pl.BlockSpec((count, pairs, degrees), lambda i: (i, 0, 0))] + leg_specs,
            out_specs=pl.BlockSpec((pairs, block), lambda i: (0, i)),
            compiler_params=params(),
            cost_estimate=legendre_cost,
            name="legendre_forward",
        )(spectral.reshape(slots, pairs, degrees), leg_rows, thr)
        coef = jnp.transpose(coef.reshape(pairs, slots, lats), (2, 0, 1))
    else:
        keep = jnp.arange(degrees, dtype=jnp.int32)[None, :] >= wave_here[:, None]
        kept = jnp.where(keep[:, None, :], legendre, jnp.zeros((), jnp.bfloat16))
        coef = jnp.einsum(
            "spn,sln->lps",
            spectral.reshape(slots, pairs, degrees),
            kept,
            preferred_element_type=jnp.float32,
        ).astype(jnp.bfloat16)
    coef = jnp.pad(coef, ((0, 0), (0, 0), (0, padded - slots)))
    local = lats // waves
    coef = lax.all_to_all(
        coef.reshape(waves, local, pairs, padded), "wave", split_axis=0, concat_axis=0, tiled=True
    )

    mix = level_mix.astype(jnp.bfloat16)
    split = fields % levels != 0
    grid_parts, back_parts = [], []
    for lat in range(local):
        x = jnp.transpose(coef[:, lat], (1, 0, 2)).reshape(pairs, waves * padded)
        x = jnp.pad(x, ((0, 0), (0, total - waves * padded)))
        points = lat_points[lat : lat + 1]
        table = make_table(table_wave, points, rows)
        group = fields
        if split:
            x = lax.all_gather(x.reshape(2, fields, total), "band", axis=1, tiled=True)
            group = fields * bands
            x = x.reshape(2 * group, total)
        scale_cols = jnp.broadcast_to(scale_all[lat][:, None], (lons, group))
        g, back = on_grid(levels, x, table, wave_row, points, mix, scale_cols, lons)
        if split:
            mine = lax.axis_index("band") * fields
            g = lax.dynamic_slice_in_dim(g, mine, fields, axis=0)
            back = lax.dynamic_slice_in_dim(
                back.reshape(2, group, total), mine, fields, axis=1
            ).reshape(pairs, total)
        grid_parts.append(g.reshape(fields, bands, lon_width))
        back_parts.append(back[:, : waves * padded].reshape(pairs, waves, padded))
    back = jnp.stack([jnp.transpose(b, (1, 0, 2)) for b in back_parts], axis=1)
    back = lax.all_to_all(back, "wave", split_axis=0, concat_axis=0, tiled=True)
    back = back.reshape(lats, pairs, padded)[:, :, :slots]
    grid = jnp.stack(grid_parts, axis=2)
    back, grid = lax.optimization_barrier((back, grid))
    grid = lax.all_to_all(grid, "band", split_axis=1, concat_axis=0, tiled=True)
    grid_out = grid.reshape(fields * bands, local, lon_width).astype(jnp.float32)

    weighted = (back.astype(jnp.float32) * gauss_w[:, None, None]).astype(jnp.bfloat16)
    if count:
        coef = jnp.transpose(weighted, (1, 2, 0)).reshape(pairs, slots * lats)
        spec_out = pl.pallas_call(
            lambda *refs: backward_kernel(lats, *refs),
            grid=(slots // count,),
            out_shape=jax.ShapeDtypeStruct((slots, pairs, degrees), jnp.bfloat16),
            in_specs=[pl.BlockSpec((pairs, block), lambda i: (0, i))] + leg_specs,
            out_specs=pl.BlockSpec((count, pairs, degrees), lambda i: (i, 0, 0)),
            compiler_params=params(),
            cost_estimate=legendre_cost,
            name="legendre_backward",
        )(coef, leg_rows, thr)
    else:
        spec_out = jnp.einsum(
            "lps,sln->spn", weighted, kept, preferred_element_type=jnp.float32
        ).astype(jnp.bfloat16)
    return grid_out, spec_out.reshape(slots, 2, fields, degrees)


def solution(mesh):
    placed = (
        P("wave", None, "band", None),
        P("wave", None, None),
        P(),
        P("wave"),
        P(),
        P("wave", "band"),
        P(),
    )
    return jax.shard_map(
        body,
        mesh=mesh,
        in_specs=placed,
        out_specs=(P(None, "wave", "band"), P("wave", None, "band", None)),
        check_vma=False,
    )
```

time: 325 us -> 122 us (0.38); the launches traced: 319 us -> 120 us
  other arithmetic: 146 us -> 1.44 us
  matrix products: 89.5 us -> 0 us
  Pallas kernels: 0 us -> 72.3 us
  blocking collectives: 49.3 us -> 5.18 us
  local copies, waits for them, and re-layouts: 11.3 us -> 15.1 us
    another operation x1 -> x0, other arithmetic: 145 us -> none  [trig_table(): return jnp.stack([jnp.cos(angle_rad), jnp.sin(angle_rad)], axis=2)]
    dot_general x5 -> x0, matrix products: 89.5 us -> none  [the longest x1 30.9 us: body(): jnp.einsum('scfn,sln->scfl', masked, legendre, preferred_element_type=jnp...]
    pallas_call x0 -> x4, Pallas kernels: none -> 72.3 us  [the longest x1 23.6 us: body(): pl.pallas_call(lambda *refs: forward_kernel(lats, *refs), grid=(slots //...]
    unnamed x1 -> x0, blocking collectives: 39.3 us -> none
    broadcast_in_dim x0 -> x4, local copies, waits for them, and re-layouts: none -> 4.9 us  [the longest x1 3.43 us: body(): scale_cols = jnp.broadcast_to(scale_all[lat][:, None], (lons, group))]
    all_gather x1, blocking collectives: 10 us -> 5.18 us  [body(): scale_all = lax.all_gather(grid_scale, 'band', axis=1, tiled=True)]
    reshape x0 -> x6, local copies, waits for them, and re-layouts: none -> 4.48 us  [the longest x1 1.67 us: body(): back_parts.append(back[:, :waves * padded].reshape(pairs, waves, padded))]
    all_to_all x2 -> x3, starting transfers between devices: 13.8 us -> 16.7 us  [the longest x1 7.25 us: body(): lax.all_to_all(coef.reshape(waves, local, pairs, padded), 'wave', split_a...]
  transfers between devices with their start and end apart: 2 -> 3, of which waited for: 1 -> 1; matrix products, arithmetic and copies ran while one was open for 46% -> 2% of each run, Pallas kernels for 0% -> 24%
where the time goes in v1:
time: 122 us; the launch traced here: 120 us
  Pallas kernels  72.3 us (59%)
  starting transfers between devices  16.7 us (14%)
  local copies, waits for them, and re-layouts  15.1 us (12%)
  waiting for transfers between devices  8.31 us (7%)
  blocking collectives  5.18 us (4%)
  other arithmetic  1.44 us (1%)
  between operations  1.39 us (1%)
    pallas_call x1, Pallas kernels, body(): pl.pallas_call(lambda *refs: forward_kernel(lats, *refs), grid=(slots //...  23.6 us
    pallas_call x1, Pallas kernels, body(): pl.pallas_call(lambda *refs: backward_kernel(lats, *refs), grid=(slots //...  20.6 us
    pallas_call x1, Pallas kernels, on_grid(): pl.pallas_call(lambda *refs: grid_kernel(levels, *refs), out_shape=(jax.S...  19.5 us
    pallas_call x1, Pallas kernels, make_table(): pl.pallas_call(lambda *refs: table_kernel(512 if slots % 512 == 0 else 12...  8.59 us
    all_to_all x1, waiting for transfers between devices, body(): back = lax.all_to_all(back, 'wave', split_axis=0, concat_axis=0, tiled=True)  8.31 us
    all_to_all x1, starting transfers between devices, body(): lax.all_to_all(coef.reshape(waves, local, pairs, padded), 'wave', split_a...  7.25 us
    all_to_all x1, starting transfers between devices, body(): back = lax.all_to_all(back, 'wave', split_axis=0, concat_axis=0, tiled=True)  5.99 us
    all_gather x1, blocking collectives, body(): scale_all = lax.all_gather(grid_scale, 'band', axis=1, tiled=True)  5.18 us
  transfers between devices with their start and end apart: 3, of which 1 were waited for; matrix products, arithmetic and copies ran while one was open for 2% of the time, Pallas kernels for 24%

profile of v1, /device:TPU:0, one launch (start us, length us, event | category | flops | bytes accessed | tf_op | source)
XLA Modules:
  0.0 120.5 jit_solution(13979854553969154822)
XLA Ops:
  0.6 0.8 dynamic_slice.3
  1.4 0.1 broadcast_in_dim.25
  1.5 0.1 broadcast_in_dim.26
  1.6 1.3 %broadcast_in_dim.27.refs_2_ = s32[1920,128]{1,0:T(8,128)} broadcast(s32[1920]{0:T(1024)S(1)} %broadcast_in_dim.26), dimensions={0} | broadcast | bytes 990720 | tf_op jit(solution)/shard_map/broadcast_in_dim | solution.py:265
  2.9 23.6 %legendre_forward.1 = bf16[64,1920]{1,0:T(8,128)(2,1)} custom-call(bf16[240,64,1280]{2,1,0:T(8,128)(2,1)} %bitcast.37, bf16[1920,1280]{1,0:T(8,128)(2,1)} %bitcast.39, s32[1920,128]{1,0:T(8,128)} %broadcast_in_dim.27.refs_2_), custom_call_target="tpu_custom_call" | custom-call | flops 5033164800 | bytes 44236800 | tf_op jit(solution)/shard_map/legendre_forward/pallas_call | solution.py:277
  26.5 1.2 %copy.17 = bf16[64,1920]{0,1:T(8,128)(2,1)S(1)} copy(bf16[64,1920]{1,0:T(8,128)(2,1)} %legendre_forward.1) | data formatting | bytes 491520 | tf_op jit(solution)/shard_map/legendre_forward/pallas_call | solution.py:277
  27.7 0.1 pad_bitcast_fusion
  27.8 1.0 copy.18
  28.8 7.3 %all-to-all-start = ((bf16[8,1,64,256]{3,2,1,0:T(8,128)(2,1)}), bf16[8,1,64,256]{3,2,1,0:T(8,128)(2,1)S(1)}, u32[]{:S(2)}, u32[]{:S(2)}) async-start(bf16[8,1,64,256]{3,2,1,0:T(8,128)(2,1)} %copy.18), calls=%async_computation | async-start | bytes 524288 | tf_op jit(solution)/shard_map/all_to_all | solution.py:299
  36.1 0.0 copy-done.1
  36.1 0.1 reshape.105
  36.9 0.6 convert_element_type.31.refs_4_
  37.5 5.2 %all_gather.3 = f32[1,5632]{1,0:T(1,128)S(1)} all-gather(f32[1,1408]{1,0:T(1,128)S(1)} %copy-done.2), channel_id=1, replica_groups=mesh['wave'=8,'band'=4] {'band'}, dimensions={1}, use_global_device_ids=true | all-gather | bytes 28160 | tf_op jit(solution)/shard_map/all_gather | solution.py:262
  42.7 0.1 reduce
  42.7 0.6 compare_select_fusion.1
  43.3 8.6 %trig_table.1.refs_1_ = bf16[1408,4096]{1,0:T(8,128)(2,1)} custom-call(s32[1,2048]{1,0:T(1,128)} %get-tuple-element.13.refs_0_, s32[1]{0:T(128)S(6)} %copy.30.refs_1_.refs_3_), custom_call_target="tpu_custom_call" | custom-call | flops 46137344 | bytes 11534336 | tf_op jit(solution)/shard_map/trig_table/pallas_call | solution.py:193
  51.9 0.0 all-to-all-done
  51.9 0.7 copy.26
  52.6 3.4 %broadcast_in_dim.31.refs_5_ = f32[5632,32]{1,0:T(8,128)} broadcast(f32[5632]{0:T(1024)S(1)} %reduce), dimensions={0} | broadcast | bytes 743424 | tf_op jit(solution)/shard_map/broadcast_in_dim | solution.py:316
  56.1 19.5 %grid_step.1 = (bf16[32,5632]{1,0:T(8,128)(2,1)}, bf16[64,2048]{1,0:T(8,128)(2,1)}) custom-call(bf16[64,2048]{1,0:T(8,128)(2,1)} %bitcast.44, bf16[1408,4096]{1,0:T(8,128)(2,1)} %trig_table.1.refs_1_, s32[1,2048]{1,0:T(1,128)} %get-tuple-element.12.refs_2_, s32[1]{0:T(128)S(6)} %copy.30.refs_1_.refs_3_, bf16[32,32]{1,0:T(8,128)(2,1)} %convert_element_type.31.refs_4_, ...), custom_call_target="tpu_custom_call" | custom-call | flops 2952790016 | bytes 11534336 | tf_op jit(solution)/shard_map/grid_step/pallas_call | solution.py:210
  75.6 1.7 %copy.29 = bf16[8,8,8,256]{3,2,0,1:T(8,128)(2,1)} copy(bf16[8,8,8,256]{3,2,1,0:T(8,128)(2,1)} %bitcast.47) | data formatting | bytes 524288 | tf_op jit(solution)/shard_map/reshape | solution.py:325
  77.2 6.0 %all-to-all-start.1 = ((bf16[8,1,64,256]{3,2,1,0:T(8,128)(2,1)}), bf16[8,1,64,256]{3,2,1,0:T(8,128)(2,1)S(1)}, u32[]{:S(2)}, u32[]{:S(2)}) async-start(bf16[8,1,64,256]{3,2,1,0:T(8,128)(2,1)} %bitcast.35), calls=%async_computation.1 | async-start | bytes 524288 | tf_op jit(solution)/shard_map/all_to_all | solution.py:327
  83.2 1.1 stack_reshape.3
  84.3 8.3 %all-to-all-done.1 = bf16[8,1,64,256]{3,2,1,0:T(8,128)(2,1)S(1)} async-done(((bf16[8,1,64,256]{3,2,1,0:T(8,128)(2,1)}), bf16[8,1,64,256]{3,2,1,0:T(8,128)(2,1)S(1)}, u32[]{:S(2)}, u32[]{:S(2)}) %all-to-all-start.1) | async-done | bytes 262176 | tf_op jit(solution)/shard_map/all_to_all | solution.py:327
  92.6 0.1 fusion
  92.7 0.3 copy.22
  93.0 0.9 copy.23.refs_0_
  93.9 0.8 copy.21
  94.7 3.5 %all-to-all-start.2 = ((bf16[32,4,1,1408]{3,0,2,1:T(8,128)(2,1)}), bf16[32,4,1,1408]{3,0,2,1:T(8,128)(2,1)S(1)}, u32[]{:S(2)}, u32[]{:S(2)}) async-start(bf16[32,4,1,1408]{3,0,2,1:T(8,128)(2,1)} %copy.21), calls=%async_computation.2 | async-start | bytes 720896 | tf_op jit(solution)/shard_map/all_to_all | solution.py:331
  98.2 20.6 %legendre_backward.1 = bf16[240,64,1280]{2,1,0:T(8,128)(2,1)} custom-call(bf16[64,1920]{1,0:T(8,128)(2,1)} %copy.23.refs_0_, bf16[1920,1280]{1,0:T(8,128)(2,1)} %bitcast.40, s32[1920,128]{1,0:T(8,128)} %broadcast_in_dim.27.refs_2_), custom_call_target="tpu_custom_call" | custom-call | flops 5033164800 | bytes 44236800 | tf_op jit(solution)/shard_map/legendre_backward/pallas_call | solution.py:337
  118.8 0.0 all-to-all-done.2
  118.9 1.6 %copy.24 = f32[128,1,1408]{2,1,0:T(1,128)} copy(f32[128,1,1408]{2,0,1:T(8,128)S(1)} %bitcast.41) | data formatting | bytes 1441792
  (10 shorter events, 0.1 us)
Async XLA Ops:
  2.9 33.2 %copy-start.1 = (s32[1920]{0:T(1024)S(1)}, s32[1920]{0:T(1024)}, u32[]{:S(2)}) copy-start(s32[1920]{0:T(1024)} %param.9) | copy-start | bytes 23044
  2.9 34.0 %copy-start = (f32[32,32]{1,0:T(8,128)S(1)}, f32[32,32]{1,0:T(8,128)}, u32[]{:S(2)}) copy-start(f32[32,32]{1,0:T(8,128)} %param.11) | copy-start | bytes 12292
  2.9 34.6 %copy-start.2 = (f32[1,1408]{1,0:T(1,128)S(1)}, f32[1,1408]{1,0:T(1,128)}, u32[]{:S(2)}) copy-start(f32[1,1408]{1,0:T(1,128)} %param.12) | copy-start | bytes 16900
  28.8 23.1 %all-to-all-start = ((bf16[8,1,64,256]{3,2,1,0:T(8,128)(2,1)}), bf16[8,1,64,256]{3,2,1,0:T(8,128)(2,1)S(1)}, u32[]{:S(2)}, u32[]{:S(2)}) async-start(bf16[8,1,64,256]{3,2,1,0:T(8,128)(2,1)} %copy.18), calls=%async_computation | async-start | bytes 524288 | tf_op jit(solution)/shard_map/all_to_all | solution.py:299
  51.9 40.7 %copy-start.3 = (f32[8]{0:T(128)S(1)}, f32[8]{0:T(128)}, u32[]{:S(2)}) copy-start(f32[8]{0:T(128)} %param.13) | copy-start | bytes 100
  77.2 15.4 %all-to-all-start.1 = ((bf16[8,1,64,256]{3,2,1,0:T(8,128)(2,1)}), bf16[8,1,64,256]{3,2,1,0:T(8,128)(2,1)S(1)}, u32[]{:S(2)}, u32[]{:S(2)}) async-start(bf16[8,1,64,256]{3,2,1,0:T(8,128)(2,1)} %bitcast.35), calls=%async_computation.1 | async-start | bytes 524288 | tf_op jit(solution)/shard_map/all_to_all | solution.py:327
  94.7 24.1 %all-to-all-start.2 = ((bf16[32,4,1,1408]{3,0,2,1:T(8,128)(2,1)}), bf16[32,4,1,1408]{3,0,2,1:T(8,128)(2,1)S(1)}, u32[]{:S(2)}, u32[]{:S(2)}) async-start(bf16[32,4,1,1408]{3,0,2,1:T(8,128)(2,1)} %copy.21), calls=%async_computation.2 | async-start | bytes 720896 | tf_op jit(solution)/shard_map/all_to_all | solution.py:331

commit v2 on v1

--- a/solution.py
+++ b/solution.py
@@ -29,7 +29,7 @@
     legm = masked_legendre(leg_ref, thr_ref)
     lane_slot = lax.broadcasted_iota(jnp.int32, (pairs, slots * lats), 1) // lats
     total = jnp.zeros((pairs, slots * lats), jnp.float32)
-    step = 4
+    step = slots
     for first in range(0, slots, step):
         block = spec_ref[first : first + step].reshape(step * pairs, degrees)
         res = dot(block, legm, NT)
@@ -43,13 +43,13 @@
     legm = masked_legendre(leg_ref, thr_ref)
     lane_slot = lax.broadcasted_iota(jnp.int32, (pairs, slots * lats), 1) // lats
     coef = coef_ref[...].astype(jnp.float32)
-    step = 4
-    for first in range(0, slots, step):
-        lhs = jnp.concatenate(
-            [jnp.where(lane_slot == first + k, coef, 0.0) for k in range(step)], axis=0
-        ).astype(jnp.bfloat16)
-        res = dot(lhs, legm, NN).astype(jnp.bfloat16)
-        out_ref[first : first + step] = res.reshape(step, pairs, degrees)
+    lhs = jnp.concatenate(
+        [jnp.where(lane_slot == k, coef, 0.0) for k in range(slots)], axis=0
+    ).astype(jnp.bfloat16)
+    width = 256 if degrees % 256 == 0 else degrees
+    for first in range(0, degrees, width):
+        res = dot(lhs, legm[:, first : first + width], NN).astype(jnp.bfloat16)
+        out_ref[:, :, first : first + width] = res.reshape(slots, pairs, width)
 
 
 def turn(product, points, inverse):
@@ -91,13 +91,24 @@
 
 
 def grid_kernel(
-    levels, coef_ref, table_ref, wave_ref, points_ref, mix_ref, scale_ref,
-    grid_ref, back_ref, canvas, groups, sums,
+    levels, coef_ref, table_hbm, wave_ref, points_ref, mix_ref, scale_ref,
+    grid_ref, back_ref, canvas, groups, sums, table_ref, arrived,
 ):
     fields = coef_ref.shape[0] // 2
     rows = table_ref.shape[0]
     slots = wave_ref.shape[1]
     lons = grid_ref.shape[1]
+    part = rows // 4
+    copies = [
+        pltpu.make_async_copy(
+            table_hbm.at[pl.ds(i * part, part)],
+            table_ref.at[pl.ds(i * part, part)],
+            arrived.at[i],
+        )
+        for i in range(4)
+    ]
+    for copy in copies:
+        copy.start()
     points = points_ref[0]
     quarter = points // 4
     wave = wave_ref[...]
@@ -118,11 +129,9 @@
         groups[at, low] = to_cos.astype(jnp.bfloat16)
         groups[at, high] = to_sin.astype(jnp.bfloat16)
 
-    part = rows // 4
-
-    @pl.loop(0, 4)
-    def _(i):
-        at = pl.ds(pl.multiple_of(i * part, 16), part)
+    for i in range(4):
+        copies[i].wait()
+        at = pl.ds(i * part, part)
         sums[at, :] = dot(table_ref[at, :], groups[...], NT)
 
     ga = sums[:, 0 * fields : 1 * fields]
@@ -132,7 +141,7 @@
     for r, x in enumerate((ga + gb, gc + gd, ga - gb, gc - gd)):
         canvas[pl.ds(r * quarter, rows), :] = x
 
-    tile = 128
+    tile = 512 if lons % 512 == 0 else 128
 
     @pl.loop(0, lons // tile)
     def _(i):
@@ -145,7 +154,7 @@
             dot(gl[:, f : f + levels], mix_ref[...], NT) for f in range(0, fields, levels)
         ]
         mixed = mixed[0] if len(mixed) == 1 else jnp.concatenate(mixed, axis=1)
-        canvas[at, :] = mixed * scale_ref[at, :]
+        canvas[at, :] = mixed * jnp.broadcast_to(scale_ref[:, at], (fields, tile)).T
 
     inside = lax.broadcasted_iota(jnp.int32, (rows, fields), 0) < quarter
     y = [jnp.where(inside, canvas[pl.ds(r * quarter, rows), :], 0.0) for r in range(4)]
@@ -203,7 +212,7 @@
     )(wave_row, points)
 
 
-def on_grid(levels, coef, table, wave_row, points, mix, scale_cols, lons):
+def on_grid(levels, coef, table, wave_row, points, mix, scale_row, lons):
     pairs, slots = coef.shape
     fields = pairs // 2
     rows = table.shape[0]
@@ -213,12 +222,16 @@
             jax.ShapeDtypeStruct((fields, lons), jnp.bfloat16),
             jax.ShapeDtypeStruct((pairs, slots), jnp.bfloat16),
         ),
-        in_specs=[whole(), whole(), whole(), scalar(), whole(), whole()],
+        in_specs=[
+            whole(), pl.BlockSpec(memory_space=pl.ANY), whole(), scalar(), whole(), whole()
+        ],
         out_specs=(whole(), whole()),
         scratch_shapes=[
             pltpu.VMEM((lons + rows, fields), jnp.float32),
             pltpu.VMEM((4 * fields, 2 * slots), jnp.bfloat16),
             pltpu.VMEM((rows, 4 * fields), jnp.float32),
+            pltpu.VMEM((rows, 2 * slots), jnp.bfloat16),
+            pltpu.SemaphoreType.DMA((4,)),
         ],
         compiler_params=params(),
         cost_estimate=pl.CostEstimate(
@@ -227,7 +240,17 @@
             transcendentals=0,
         ),
         name="grid_step",
-    )(coef, table, wave_row, points, mix, scale_cols)
+    )(coef, table, wave_row, points, mix, scale_row)
+
+
+def gather_rows(x, bands):
+    me = lax.axis_index("band")
+    parts = [x]
+    for k in range(1, bands):
+        parts.append(lax.ppermute(x, "band", [((d + k) % bands, d) for d in range(bands)]))
+    turned = jnp.concatenate(parts + parts, axis=1)
+    start = lax.rem(bands - me, bands) * x.shape[1]
+    return lax.dynamic_slice_in_dim(turned, start, bands * x.shape[1], axis=1)
 
 
 def block_slots(slots, lats):
@@ -259,7 +282,7 @@
     wave_row = jnp.pad(spread, ((0, 0), (0, total - waves * padded)), constant_values=empty)
     wave_row = jnp.where(wave_row >= empty, 4 * lons, wave_row)
     table_wave = jnp.where(wave_row >= 4 * lons, 0, wave_row)
-    scale_all = lax.all_gather(grid_scale, "band", axis=1, tiled=True)
+    scale_all = gather_rows(grid_scale, bands)
 
     if count:
         thr = jnp.broadcast_to(wave_here[:, None, None], (slots, lats, 128)).reshape(-1, 128)
@@ -313,8 +336,7 @@
             x = lax.all_gather(x.reshape(2, fields, total), "band", axis=1, tiled=True)
             group = fields * bands
             x = x.reshape(2 * group, total)
-        scale_cols = jnp.broadcast_to(scale_all[lat][:, None], (lons, group))
-        g, back = on_grid(levels, x, table, wave_row, points, mix, scale_cols, lons)
+        g, back = on_grid(levels, x, table, wave_row, points, mix, scale_all[lat : lat + 1], lons)
         if split:
             mine = lax.axis_index("band") * fields
             g = lax.dynamic_slice_in_dim(g, mine, fields, axis=0)

time: 122 us -> 113 us (0.926)
  blocking collectives: 5.18 us -> 0 us
  Pallas kernels: 72.3 us -> 68.8 us
  local copies, waits for them, and re-layouts: 15.1 us -> 12.4 us
  starting transfers between devices: 16.7 us -> 18.5 us
    all_gather x1 -> x0, blocking collectives: 5.18 us -> none  [body(): scale_all = lax.all_gather(grid_scale, 'band', axis=1, tiled=True)]
    pallas_call x1, Pallas kernels: 19.5 us -> 15.9 us  [on_grid(): pl.pallas_call(lambda *refs: grid_kernel(levels, *refs), out_shape=(jax.S...]
    broadcast_in_dim x1 -> x0, local copies, waits for them, and re-layouts: 3.43 us -> none  [body(): scale_cols = jnp.broadcast_to(scale_all[lat][:, None], (lons, group))]
    ppermute x0 -> x3, starting transfers between devices: none -> 3.26 us  [gather_rows(): lax.ppermute(x, 'band', [((d + k) % bands, d) for d in range(bands)])]
    all_to_all x1, starting transfers between devices: 7.25 us -> 5.8 us  [body(): lax.all_to_all(coef.reshape(waves, local, pairs, padded), 'wave', split_a...]
  transfers between devices with their start and end apart: 3 -> 6, of which waited for: 1 -> 1; matrix products, arithmetic and copies ran while one was open for 2% -> 7% of each run, Pallas kernels for 24% -> 47%
where the time goes in v2:
time: 113 us; the launch traced here: 111 us
  Pallas kernels  68.8 us (61%)
  starting transfers between devices  18.5 us (16%)
  local copies, waits for them, and re-layouts  12.4 us (11%)
  waiting for transfers between devices  8.79 us (8%)
  between operations  1.46 us (1%)
  other arithmetic  1.37 us (1%)
    pallas_call x1, Pallas kernels, body(): pl.pallas_call(lambda *refs: forward_kernel(lats, *refs), grid=(slots //...  23.7 us
    pallas_call x1, Pallas kernels, body(): pl.pallas_call(lambda *refs: backward_kernel(lats, *refs), grid=(slots //...  20.6 us
    pallas_call x1, Pallas kernels, on_grid(): pl.pallas_call(lambda *refs: grid_kernel(levels, *refs), out_shape=(jax.S...  15.9 us
    all_to_all x1, waiting for transfers between devices, body(): back = lax.all_to_all(back, 'wave', split_axis=0, concat_axis=0, tiled=True)  8.78 us
    pallas_call x1, Pallas kernels, make_table(): pl.pallas_call(lambda *refs: table_kernel(512 if slots % 512 == 0 else 12...  8.59 us
    all_to_all x1, starting transfers between devices, body(): back = lax.all_to_all(back, 'wave', split_axis=0, concat_axis=0, tiled=True)  5.99 us
    all_to_all x1, starting transfers between devices, body(): lax.all_to_all(coef.reshape(waves, local, pairs, padded), 'wave', split_a...  5.8 us
    all_to_all x1, starting transfers between devices, body(): grid = lax.all_to_all(grid, 'band', split_axis=1, concat_axis=0, tiled=True)  3.46 us
  transfers between devices with their start and end apart: 6, of which 1 were waited for; matrix products, arithmetic and copies ran while one was open for 7% of the time, Pallas kernels for 47%

profile of v2, /device:TPU:0, one launch (start us, length us, event | category | flops | bytes accessed | tf_op | source)
XLA Modules:
  0.0 111.4 jit_solution(1738326886264294647)
XLA Ops:
  0.7 2.5 %collective-permute-start = (f32[1,1408]{1,0:T(1,128)}, f32[1,1408]{1,0:T(1,128)S(1)}, u32[]{:S(2)}, u32[]{:S(2)}) collective-permute-start(f32[1,1408]{1,0:T(1,128)} %param.12), channel_id=1, source_target_pairs={{1,0},{2,1},{3,2},{0,3},{5,4},{6,5},{7,6},{4,7},{9,8},{10,9},{11,1... | collective-permute-start | bytes 16904 | tf_op jit(solution)/shard_map/ppermute | solution.py:250
  3.1 0.6 collective-permute-start.1
  3.8 0.2 collective-permute-start.2
  3.9 0.8 dynamic_slice.6
  4.7 0.1 broadcast_in_dim.18
  4.8 0.1 broadcast_in_dim.19
  4.9 1.3 %broadcast_in_dim.20.refs_2_ = s32[1920,128]{1,0:T(8,128)} broadcast(s32[1920]{0:T(1024)S(1)} %broadcast_in_dim.19), dimensions={0} | broadcast | bytes 990720 | tf_op jit(solution)/shard_map/broadcast_in_dim | solution.py:288
  6.2 23.7 %legendre_forward.1 = bf16[64,1920]{1,0:T(8,128)(2,1)} custom-call(bf16[240,64,1280]{2,1,0:T(8,128)(2,1)} %bitcast.37, bf16[1920,1280]{1,0:T(8,128)(2,1)} %bitcast.39, s32[1920,128]{1,0:T(8,128)} %broadcast_in_dim.20.refs_2_), custom_call_target="tpu_custom_call" | custom-call | flops 5033164800 | bytes 44236800 | tf_op jit(solution)/shard_map/legendre_forward/pallas_call | solution.py:300
  29.9 1.2 %copy.17 = bf16[64,1920]{0,1:T(8,128)(2,1)S(1)} copy(bf16[64,1920]{1,0:T(8,128)(2,1)} %legendre_forward.1) | data formatting | bytes 491520 | tf_op jit(solution)/shard_map/legendre_forward/pallas_call | solution.py:300
  31.1 0.1 pad_bitcast_fusion
  31.2 1.0 copy.18
  32.2 5.8 %all-to-all-start = ((bf16[8,1,64,256]{3,2,1,0:T(8,128)(2,1)}), bf16[8,1,64,256]{3,2,1,0:T(8,128)(2,1)S(1)}, u32[]{:S(2)}, u32[]{:S(2)}) async-start(bf16[8,1,64,256]{3,2,1,0:T(8,128)(2,1)} %copy.18), calls=%async_computation | async-start | bytes 524288 | tf_op jit(solution)/shard_map/all_to_all | solution.py:322
  38.0 0.1 reshape.104
  38.1 0.6 compare_select_fusion.1
  39.4 0.6 convert_element_type.31.refs_4_
  40.0 8.6 %trig_table.1.refs_1_ = bf16[1408,4096]{1,0:T(8,128)(2,1)} custom-call(s32[1,2048]{1,0:T(1,128)} %get-tuple-element.13.refs_0_, s32[1]{0:T(128)S(6)} %copy.37.refs_1_.refs_3_), custom_call_target="tpu_custom_call" | custom-call | flops 46137344 | bytes 11534336 | tf_op jit(solution)/shard_map/trig_table/pallas_call | solution.py:202
  48.6 0.0 collective-permute-done
  48.7 0.6 constant_dynamic-slice_fusion.refs_5_
  49.3 0.0 all-to-all-done
  49.3 0.7 copy.26
  50.1 15.9 %grid_step.1 = (bf16[32,5632]{1,0:T(8,128)(2,1)}, bf16[64,2048]{1,0:T(8,128)(2,1)}) custom-call(bf16[64,2048]{1,0:T(8,128)(2,1)} %bitcast.44, bf16[1408,4096]{1,0:T(8,128)(2,1)} %trig_table.1.refs_1_, s32[1,2048]{1,0:T(1,128)} %get-tuple-element.12.refs_2_, s32[1]{0:T(128)S(6)} %copy.37.refs_1_.refs_3_, bf16[32,32]{1,0:T(8,128)(2,1)} %convert_element_type.31.refs_4_, ...), custom_call_target="tpu_custom_call" | custom-call | flops 2952790016 | bytes 11534336 | tf_op jit(solution)/shard_map/grid_step/pallas_call | solution.py:219
  66.0 1.7 %copy.29 = bf16[8,8,8,256]{3,2,0,1:T(8,128)(2,1)} copy(bf16[8,8,8,256]{3,2,1,0:T(8,128)(2,1)} %bitcast.47) | data formatting | bytes 524288 | tf_op jit(solution)/shard_map/reshape | solution.py:347
  67.7 6.0 %all-to-all-start.1 = ((bf16[8,1,64,256]{3,2,1,0:T(8,128)(2,1)}), bf16[8,1,64,256]{3,2,1,0:T(8,128)(2,1)S(1)}, u32[]{:S(2)}, u32[]{:S(2)}) async-start(bf16[8,1,64,256]{3,2,1,0:T(8,128)(2,1)} %bitcast.35), calls=%async_computation.1 | async-start | bytes 524288 | tf_op jit(solution)/shard_map/all_to_all | solution.py:349
  73.7 1.1 stack_reshape.3
  74.7 8.8 %all-to-all-done.1 = bf16[8,1,64,256]{3,2,1,0:T(8,128)(2,1)S(1)} async-done(((bf16[8,1,64,256]{3,2,1,0:T(8,128)(2,1)}), bf16[8,1,64,256]{3,2,1,0:T(8,128)(2,1)S(1)}, u32[]{:S(2)}, u32[]{:S(2)}) %all-to-all-start.1) | async-done | bytes 262176 | tf_op jit(solution)/shard_map/all_to_all | solution.py:349
  83.5 0.1 fusion
  83.6 0.3 copy.22
  83.9 0.9 copy.23.refs_0_
  84.8 0.8 copy.21
  85.6 3.5 %all-to-all-start.2 = ((bf16[32,4,1,1408]{3,0,2,1:T(8,128)(2,1)}), bf16[32,4,1,1408]{3,0,2,1:T(8,128)(2,1)S(1)}, u32[]{:S(2)}, u32[]{:S(2)}) async-start(bf16[32,4,1,1408]{3,0,2,1:T(8,128)(2,1)} %copy.21), calls=%async_computation.2 | async-start | bytes 720896 | tf_op jit(solution)/shard_map/all_to_all | solution.py:353
  89.1 20.6 %legendre_backward.1 = bf16[240,64,1280]{2,1,0:T(8,128)(2,1)} custom-call(bf16[64,1920]{1,0:T(8,128)(2,1)} %copy.23.refs_0_, bf16[1920,1280]{1,0:T(8,128)(2,1)} %bitcast.40, s32[1920,128]{1,0:T(8,128)} %broadcast_in_dim.20.refs_2_), custom_call_target="tpu_custom_call" | custom-call | flops 5033164800 | bytes 44236800 | tf_op jit(solution)/shard_map/legendre_backward/pallas_call | solution.py:359
  109.8 1.6 %copy.24 = f32[128,1,1408]{2,1,0:T(1,128)} copy(f32[128,1,1408]{2,0,1:T(8,128)S(1)} %bitcast.41) | data formatting | bytes 1441792
  (22 shorter events, 0.2 us)
Async XLA Ops:
  0.6 38.1 %copy-start = (f32[1,1408]{1,0:T(1,128)S(1)}, f32[1,1408]{1,0:T(1,128)}, u32[]{:S(2)}) copy-start(f32[1,1408]{1,0:T(1,128)} %param.12) | copy-start | bytes 16900
  0.6 37.4 %copy-start.2 = (s32[1920]{0:T(1024)S(1)}, s32[1920]{0:T(1024)}, u32[]{:S(2)}) copy-start(s32[1920]{0:T(1024)} %param.9) | copy-start | bytes 23044
  0.7 38.8 %copy-start.1 = (f32[32,32]{1,0:T(8,128)S(1)}, f32[32,32]{1,0:T(8,128)}, u32[]{:S(2)}) copy-start(f32[32,32]{1,0:T(8,128)} %param.11) | copy-start | bytes 12292
  0.7 82.9 %copy-start.3 = (f32[8]{0:T(128)S(1)}, f32[8]{0:T(128)}, u32[]{:S(2)}) copy-start(f32[8]{0:T(128)} %param.13) | copy-start | bytes 100
  0.7 47.9 %collective-permute-start = (f32[1,1408]{1,0:T(1,128)}, f32[1,1408]{1,0:T(1,128)S(1)}, u32[]{:S(2)}, u32[]{:S(2)}) collective-permute-start(f32[1,1408]{1,0:T(1,128)} %param.12), channel_id=1, source_target_pairs={{1,0},{2,1},{3,2},{0,3},{5,4},{6,5},{7,6},{4,7},{9,8},{10,9},{11,1... | collective-permute-start | bytes 16904 | tf_op jit(solution)/shard_map/ppermute | solution.py:250
  3.1 45.5 %collective-permute-start.1 = (f32[1,1408]{1,0:T(1,128)}, f32[1,1408]{1,0:T(1,128)S(1)}, u32[]{:S(2)}, u32[]{:S(2)}) collective-permute-start(f32[1,1408]{1,0:T(1,128)} %param.12), channel_id=1, source_target_pairs={{2,0},{3,1},{0,2},{1,3},{6,4},{7,5},{4,6},{5,7},{10,8},{11,9},{8,1... | collective-permute-start | bytes 16904 | tf_op jit(solution)/shard_map/ppermute | solution.py:250
  3.8 44.9 %collective-permute-start.2 = (f32[1,1408]{1,0:T(1,128)}, f32[1,1408]{1,0:T(1,128)S(1)}, u32[]{:S(2)}, u32[]{:S(2)}) collective-permute-start(f32[1,1408]{1,0:T(1,128)} %param.12), channel_id=1, source_target_pairs={{3,0},{0,1},{1,2},{2,3},{7,4},{4,5},{5,6},{6,7},{11,8},{8,9},{9,10... | collective-permute-start | bytes 16904 | tf_op jit(solution)/shard_map/ppermute | solution.py:250
  32.2 17.1 %all-to-all-start = ((bf16[8,1,64,256]{3,2,1,0:T(8,128)(2,1)}), bf16[8,1,64,256]{3,2,1,0:T(8,128)(2,1)S(1)}, u32[]{:S(2)}, u32[]{:S(2)}) async-start(bf16[8,1,64,256]{3,2,1,0:T(8,128)(2,1)} %copy.18), calls=%async_computation | async-start | bytes 524288 | tf_op jit(solution)/shard_map/all_to_all | solution.py:322
  67.7 15.9 %all-to-all-start.1 = ((bf16[8,1,64,256]{3,2,1,0:T(8,128)(2,1)}), bf16[8,1,64,256]{3,2,1,0:T(8,128)(2,1)S(1)}, u32[]{:S(2)}, u32[]{:S(2)}) async-start(bf16[8,1,64,256]{3,2,1,0:T(8,128)(2,1)} %bitcast.35), calls=%async_computation.1 | async-start | bytes 524288 | tf_op jit(solution)/shard_map/all_to_all | solution.py:349
  85.6 24.1 %all-to-all-start.2 = ((bf16[32,4,1,1408]{3,0,2,1:T(8,128)(2,1)}), bf16[32,4,1,1408]{3,0,2,1:T(8,128)(2,1)S(1)}, u32[]{:S(2)}, u32[]{:S(2)}) async-start(bf16[32,4,1,1408]{3,0,2,1:T(8,128)(2,1)} %copy.21), calls=%async_computation.2 | async-start | bytes 720896 | tf_op jit(solution)/shard_map/all_to_all | solution.py:353
